TPU v7x, 32 devices: a whole 2x2x4 slice. The times are simulated.
32 devices in a mesh: groups: 2 (over y), ha: 4 (over z), ta: 2 (over x), col: 2 (over core).
Axes of the slice: x: 2, y: 2, z: 4, core: 2. Of those that a mesh axis runs over, the one named last changes fastest.
Arguments:
- tokens: bfloat16 [8, 16, 64, 768], P(('groups', 'ta'), 'ha', None, 'col'), parts along dimension 0, may hold values from -6 to 6
- norm1_gain: float32 [768], replicated, may hold values from 0.4 to 1.6
- w_qkv: bfloat16 [3, 768, 768], P(None, None, 'col'), may hold values from -0.21875 to 0.21875
- w_out: bfloat16 [768, 768], P('col'), may hold values from -0.3125 to 0.3125
- norm2_gain: float32 [768], replicated, may hold values from 0.4 to 1.6
- w_up: bfloat16 [768, 3072], P('ha', 'col'), may hold values from -0.21875 to 0.21875
- w_down: bfloat16 [3072, 768], P('col', 'ha'), may hold values from -0.109375 to 0.109375
Outputs:
- block_out: bfloat16 [8, 16, 64, 768], P(('groups', 'ta'), 'ha', None, 'col'), parts along dimension 0
There are 2 independent parts, one for each index of `groups`. A program takes and returns all parts, laid end to end along the dimension named above; an argument that names none is the same for every part. Nothing has to cross between parts.
All inputs are finite; a program needn't handle non-finite values.
Results may differ from a plain program's by a relative error of at most 0.009.
Values may be sent and summed in bfloat16 or wider, within the bound.
A program may use at most 64 MiB of HBM per device.

v0:
```python
import math
import jax
import jax.numpy as jnp
from jax import lax
from jax.sharding import PartitionSpec as P

HD = 64
EPS = 1e-05


def layer_norm(values, gain):
    mean = jnp.mean(values, -1, keepdims=True)
    centred = values - mean
    spread = jnp.mean(centred * centred, -1, keepdims=True)
    return centred * lax.rsqrt(spread + EPS) * gain


def attend(query, keys, values, dim):
    scale = 1.0 / math.sqrt(HD)
    moved_q = jnp.moveaxis(query, dim, -2)
    moved_k = jnp.moveaxis(keys, dim, -2)
    moved_v = jnp.moveaxis(values, dim, -2)
    shape = moved_q.shape
    split = shape[:-1] + (shape[-1] // HD, HD)
    scores = (
        jnp.einsum(
            "...qhd,...khd->...hqk",
            moved_q.reshape(split),
            moved_k.reshape(split),
            preferred_element_type=jnp.float32,
        )
        * scale
    )
    weights = jnp.exp(scores)
    weights = (weights / jnp.sum(weights, -1, keepdims=True)).astype(jnp.bfloat16)
    result = jnp.einsum(
        "...hqk,...khd->...qhd", weights, moved_v.reshape(split), preferred_element_type=jnp.float32
    ).astype(jnp.bfloat16)
    return jnp.moveaxis(result.reshape(shape), -2, dim)


def on_device(tokens, norm1_gain, w_qkv, w_out, norm2_gain, w_up, w_down):
    whole = lax.all_gather(tokens, "col", axis=3, tiled=True)
    frames, rows_h, width, model = whole.shape
    count = frames * rows_h * width
    half = tokens.shape[3]
    wide = whole.astype(jnp.float32).reshape(count, model)
    normed = layer_norm(wide, norm1_gain).astype(jnp.bfloat16)
    stacked = jnp.einsum("rd,sdc->src", normed, w_qkv, preferred_element_type=jnp.float32).astype(
        jnp.bfloat16
    )
    stacked = stacked.reshape(3, frames, rows_h, width, half)
    along_w = attend(stacked[0], stacked[1], stacked[2], 2)
    columns = lax.all_to_all(stacked, "ha", split_axis=3, concat_axis=2, tiled=True)
    along_h_far = attend(columns[0], columns[1], columns[2], 1)
    along_h = lax.all_to_all(along_h_far, "ha", split_axis=1, concat_axis=2, tiled=True)
    lines = lax.all_to_all(stacked, "ta", split_axis=3, concat_axis=1, tiled=True)
    along_t_far = attend(lines[0], lines[1], lines[2], 0)
    along_t = lax.all_to_all(along_t_far, "ta", split_axis=0, concat_axis=2, tiled=True)
    mixed = (
        along_w.astype(jnp.float32) + along_h.astype(jnp.float32) + along_t.astype(jnp.float32)
    ).astype(jnp.bfloat16)
    terms = jnp.dot(mixed.reshape(count, half), w_out, preferred_element_type=jnp.float32)
    offset = lax.axis_index("col") * half
    summed = lax.psum(terms, "col")
    first_full = wide + summed
    second = layer_norm(first_full, norm2_gain).astype(jnp.bfloat16)
    first = lax.dynamic_slice_in_dim(first_full, offset, half, 1)
    upper = jnp.dot(
        second, lax.all_gather(w_up, "ha", axis=0, tiled=True), preferred_element_type=jnp.float32
    )
    hidden = jax.nn.gelu(upper, approximate=False).astype(jnp.bfloat16)
    down_terms = jnp.dot(
        hidden, lax.all_gather(w_down, "ha", axis=1, tiled=True), preferred_element_type=jnp.float32
    )
    down_share = lax.psum_scatter(
        down_terms.astype(jnp.bfloat16), "col", scatter_dimension=1, tiled=True
    ).astype(jnp.float32)
    return (first + down_share).astype(jnp.bfloat16).reshape(frames, rows_h, width, half)


def solution(mesh):
    placed = (
        P(("groups", "ta"), "ha", None, "col"),
        P(),
        P(None, None, "col"),
        P("col", None),
        P(),
        P("ha", "col"),
        P("col", "ha"),
    )
    return jax.shard_map(
        on_device,
        mesh=mesh,
        in_specs=placed,
        out_specs=P(("groups", "ta"), "ha", None, "col"),
        check_vma=False,
    )
```

profile of v0, /device:TPU:0, one launch (start us, length us, event | category | flops | bytes accessed | tf_op | source)
XLA Modules:
  0.0 270.8 jit_solution(178408443112723178)
XLA Ops:
  7.4 2.8 %all_gather.9 = bf16[2,4,64,768]{3,2,1,0:T(8,128)(2,1)S(1)} all-gather(bf16[2,4,64,384]{3,2,1,0:T(8,128)(2,1)} %param.7), channel_id=1, replica_groups=mesh['groups'=2,'ha'=4,'ta'=2,'col'=2] {'col'}, dimensions={3}, use_global_device_ids=true | all-gather | bytes 1179648 | tf_op jit(solution)/shard_map/all_gather | solution.py:43
  15.4 19.9 %all_to_all.48 = bf16[3,2,4,64,384]{4,2,1,0,3:T(4,128)(2,1)} all-to-all(bf16[3,2,4,64,384]{4,2,1,0,3:T(4,128)(2,1)S(1)} %copy.127), channel_id=1, replica_groups=mesh['groups'=2,'ha'=4,'ta'=2,'col'=2] {'ta'}, dimensions={3} | all-to-all | bytes 2359296 | tf_op jit(solution)/shard_map/all_to_all | solution.py:57
  35.3 5.1 %all-to-all-start = ((bf16[3,2,4,64,384]{4,2,1,0,3:T(4,128)(2,1)}), bf16[3,2,4,64,384]{4,2,1,0,3:T(4,128)(2,1)}, u32[]{:S(2)}, u32[]{:S(2)}) async-start(bf16[3,2,4,64,384]{4,2,1,0,3:T(4,128)(2,1)} %copy-done.1), calls=%async_computation | async-start | bytes 2359296 | tf_op jit(solution)/shard_map/all_to_all | solution.py:54
  40.4 2.1 fusion.92
  42.5 2.4 reshape.133
  49.6 2.4 reshape.139
  53.8 2.4 reshape.140
  56.2 3.9 %fusion.23 = f32[4,32,6,4,4]{3,4,2,1,0:T(4,128)} fusion(bf16[4,32,4,6,64]{4,3,1,0,2:T(8,128)(2,1)} %reshape.140, bf16[4,32,4,6,64]{4,3,1,0,2:T(8,128)(2,1)} %reshape.139), kind=kOutput, calls=%fused_computation.46 | convolution fusion | flops 1572864 | bytes 835584 | tf_op jit(solution)/shard_map/...qhd,...khd->...hqk/dot_general | solution.py:26
  60.1 1.9 copy.154
  62.9 2.3 copy.156
  66.0 2.4 reshape.138
  68.4 2.4 fusion.21
  74.7 4.4 %all-to-all-start.3 = ((bf16[4,4,32,384]{3,2,1,0:T(8,128)(2,1)}), bf16[4,4,32,384]{3,2,1,0:T(8,128)(2,1)}, u32[]{:S(2)}, u32[]{:S(2)}) async-start(bf16[4,4,32,384]{3,2,1,0:T(8,128)(2,1)} %copy.158), calls=%async_computation.3 | async-start | bytes 786432 | tf_op jit(solution)/shard_map/all_to_all | solution.py:59
  82.2 2.4 reshape.136
  86.4 2.4 reshape.137
  89.6 2.4 reshape.135
  92.1 3.8 %multiply_exponential_fusion = f32[2,16,6,16,16]{3,4,2,1,0:T(8,128)} fusion(bf16[2,16,16,6,64]{4,3,1,2,0:T(8,128)(2,1)} %reshape.137, bf16[2,16,16,6,64]{4,3,1,2,0:T(8,128)(2,1)} %reshape.136), kind=kOutput, calls=%fused_computation.32 | convolution fusion | flops 6340608 | bytes 983040 | tf_op jit(solution)/shard_map/...qhd,...khd->...hqk/dot_general | solution.py:26
  95.9 3.9 %fusion.20 = bf16[2,16,16,6,64]{4,2,3,1,0:T(8,128)(2,1)} fusion(f32[2,16,6,16,16]{3,4,2,1,0:T(8,128)} %multiply_exponential_fusion, bf16[2,16,16,6,64]{4,3,1,2,0:T(8,128)(2,1)} %reshape.135), kind=kOutput, calls=%fused_computation.41 | convolution fusion | flops 6589455 | bytes 983040 | tf_op jit(solution)/shard_map/...hqk,...khd->...qhd/dot_general | solution.py:36
  99.8 2.4 copy.139
  104.9 5.1 %all-to-all-start.1 = ((bf16[2,16,16,384]{3,2,0,1:T(8,128)(2,1)}), bf16[2,16,16,384]{3,2,0,1:T(8,128)(2,1)}, u32[]{:S(2)}, u32[]{:S(2)}) async-start(bf16[2,16,16,384]{3,2,0,1:T(8,128)(2,1)} %copy.140), calls=%async_computation.1 | async-start | bytes 786432 | tf_op jit(solution)/shard_map/all_to_all | solution.py:56
  110.0 3.3 %multiply_exponential_fusion.1 = f32[2,4,6,64,64]{3,4,2,1,0:T(8,128)} fusion(bf16[2,4,64,6,64]{4,3,2,1,0:T(8,128)(2,1)} %reshape.134, bf16[2,4,64,6,64]{4,3,2,1,0:T(8,128)(2,1)} %reshape.133), kind=kOutput, calls=%fused_computation.34 | convolution fusion | flops 25362432 | bytes 1572864 | tf_op jit(solution)/shard_map/...qhd,...khd->...hqk/dot_general | solution.py:26
  114.8 3.8 %convert_bitcast_fusion = f32[2,4,64,6,64]{2,4,3,1,0:T(8,128)} fusion(f32[2,4,6,64,64]{3,4,2,1,0:T(8,128)} %multiply_exponential_fusion.1, bf16[2,4,64,6,64]{4,3,2,1,0:T(8,128)(2,1)} %reshape.132), kind=kOutput, calls=%fused_computation.28 | convolution fusion | flops 25955392 | bytes 1966080 | tf_op jit(solution)/shard_map/...hqk,...khd->...qhd/dot_general | solution.py:36
  118.6 3.6 %copy.126 = f32[2,4,64,6,64]{2,1,0,4,3:T(4,128)} copy(f32[2,4,64,6,64]{2,4,3,1,0:T(8,128)} %convert_bitcast_fusion) | data formatting | bytes 1572864 | tf_op jit(solution)/shard_map/convert_element_type | solution.py:61
  122.2 3.1 %reshape.126 = f32[512,384]{0,1:T(8,128)} reshape(f32[2,4,64,6,64]{2,1,0,4,3:T(4,128)} %copy.126) | data formatting | bytes 1572864 | tf_op jit(solution)/shard_map/convert_element_type | solution.py:61
  130.0 3.6 %fusion.44 = f32[512,768]{1,0:T(8,128)} fusion(bf16[384,768]{1,0:T(8,128)(2,1)} %param.10, f32[512,384]{0,1:T(8,128)} %copy.160, f32[512,384]{0,1:T(8,128)} %reshape.126, f32[512,384]{0,1:T(8,128)} %copy.143), kind=kOutput, calls=%fused_computation.64 | convolution fusion | flops 302579712 | bytes 4521984 | tf_op jit(solution)/shard_map/dot_general | solution.py:63
  135.1 20.9 %all-reduce.2.cloned.1.call-done = f32[512,768]{1,0:T(8,128)} async-done(((f32[512,768]{1,0:T(8,128)}), f32[512,768]{1,0:T(8,128)}) %all-reduce.2.cloned.1.call-update) | async-done | bytes 1572880 | tf_op jit(solution)/shard_map/psum | solution.py:65
  159.1 28.4 %all-gather.3.cloned.1.call-done = bf16[768,1536]{1,0:T(8,128)(2,1)} async-done(((bf16[192,1536]{1,0:T(8,128)(2,1)}), bf16[768,1536]{1,0:T(8,128)(2,1)}) %all-gather.3.cloned.1.call-update) | async-done | bytes 2359312 | tf_op jit(solution)/shard_map/all_gather | solution.py:70
  187.6 50.3 %all-gather.5.cloned.1.call-done = bf16[1536,768]{0,1:T(8,128)(2,1)} async-done(((bf16[1536,192]{0,1:T(8,128)(2,1)}), bf16[1536,768]{0,1:T(8,128)(2,1)}) %all-gather.5.cloned.1.call-update) | async-done | bytes 2359312 | tf_op jit(solution)/shard_map/all_gather | solution.py:74
  237.8 12.3 %fusion.17 = bf16[512,768]{1,0:T(8,128)(2,1)} fusion(bf16[1536,768]{0,1:T(8,128)(2,1)} %all-gather.5.cloned.1.call-done, bf16[768,1536]{1,0:T(8,128)(2,1)} %all-gather.3.cloned.1.call-done, f32[512,768]{1,0:T(8,128)} %copy-done.2, f32[768]{0:T(1024)S(1)} %copy-done.6, f32[512]{0:T(512)S(1)} %add_rsqrt_fusion.1, f32[512]{0:T(512)S(1)} %broadcast_multiply_fusion.1), kind=kOutput, calls=%fused_computation.37 | convolution fusion | flops 2469003264 | bytes 7085056 | tf_op jit(solution)/shard_map/dot_general | solution.py:73
  250.1 2.4 copy.181
  252.6 7.0 %reduce-scatter.4.cloned.1.call-done = bf16[384,512]{1,0:T(8,128)(2,1)} async-done(((bf16[768,512]{1,0:T(8,128)(2,1)}), bf16[384,512]{1,0:T(8,128)(2,1)}) %reduce-scatter.4.cloned.1.call-update) | async-done | bytes 393232
  259.6 1.9 copy.182
  (65 shorter events, 38.3 us)
Async XLA Ops:
  7.4 3.8 %copy-start = (bf16[3,768,384]{2,1,0:T(8,128)(2,1)S(1)}, bf16[3,768,384]{2,1,0:T(8,128)(2,1)}, u32[]{:S(2)}) copy-start(bf16[3,768,384]{2,1,0:T(8,128)(2,1)} %param.9) | copy-start | bytes 5308420
  7.4 3.5 %copy-start.5 = (f32[768]{0:T(1024)S(1)}, f32[768]{0:T(1024)}, u32[]{:S(2)}) copy-start(f32[768]{0:T(1024)} %param.8) | copy-start | bytes 9220
  12.4 1.0 copy-start.4
  14.4 1.0 copy-start.1
  35.3 39.4 %all-to-all-start = ((bf16[3,2,4,64,384]{4,2,1,0,3:T(4,128)(2,1)}), bf16[3,2,4,64,384]{4,2,1,0,3:T(4,128)(2,1)}, u32[]{:S(2)}, u32[]{:S(2)}) async-start(bf16[3,2,4,64,384]{4,2,1,0,3:T(4,128)(2,1)} %copy-done.1), calls=%async_computation | async-start | bytes 2359296 | tf_op jit(solution)/shard_map/all_to_all | solution.py:54
  74.7 30.2 %all-to-all-start.3 = ((bf16[4,4,32,384]{3,2,1,0:T(8,128)(2,1)}), bf16[4,4,32,384]{3,2,1,0:T(8,128)(2,1)}, u32[]{:S(2)}, u32[]{:S(2)}) async-start(bf16[4,4,32,384]{3,2,1,0:T(8,128)(2,1)} %copy.158), calls=%async_computation.3 | async-start | bytes 786432 | tf_op jit(solution)/shard_map/all_to_all | solution.py:59
  104.9 22.8 %all-to-all-start.1 = ((bf16[2,16,16,384]{3,2,0,1:T(8,128)(2,1)}), bf16[2,16,16,384]{3,2,0,1:T(8,128)(2,1)}, u32[]{:S(2)}, u32[]{:S(2)}) async-start(bf16[2,16,16,384]{3,2,0,1:T(8,128)(2,1)} %copy.140), calls=%async_computation.1 | async-start | bytes 786432 | tf_op jit(solution)/shard_map/all_to_all | solution.py:56
  110.0 46.1 %all-reduce.2.cloned.1.call-start = ((), (), s32[]{:S(2)}) async-start(), calls=%async_computation.5 | async-start | bytes 3145728 | tf_op jit(solution)/shard_map/psum | solution.py:65
  133.7 53.9 %all-gather.3.cloned.1.call-start = ((), (), s32[]{:S(2)}) async-start(), calls=%async_computation.6 | async-start | bytes 2949120 | tf_op jit(solution)/shard_map/all_gather | solution.py:70
  134.2 103.6 %all-gather.5.cloned.1.call-start = ((), (), s32[]{:S(2)}) async-start(), calls=%async_computation.7 | async-start | bytes 2949120 | tf_op jit(solution)/shard_map/all_gather | solution.py:74
  134.8 103.0 %copy-start.6 = (f32[768]{0:T(1024)S(1)}, f32[768]{0:T(1024)}, u32[]{:S(2)}) copy-start(f32[768]{0:T(1024)} %param.11) | copy-start | bytes 9220
  134.8 124.8 %reduce-scatter.4.cloned.1.call-start = ((), (), s32[]{:S(2)}) async-start(), calls=%async_computation.8 | async-start | bytes 1179648
  157.7 1.2 copy-start.2
  250.1 11.4 %copy-start.3 = (f32[512,768]{1,0:T(8,128)S(1)}, f32[512,768]{1,0:T(8,128)}, u32[]{:S(2)}) copy-start(f32[512,768]{1,0:T(8,128)} %copy-done.2) | copy-start | bytes 4718596
Sparse Core Ops, SparseCore 0:
  133.8 22.2 all-reduce.1
  252.7 6.8 reduce-scatter.3
Sparse Core Ops, SparseCore 1:
  135.8 51.7 all-gather.2
  189.1 48.7 all-gather.4
where the time goes:
time: 272 us; the launch traced here: 271 us
  waiting for transfers between devices  108 us (40%)
  local copies, waits for them, and re-layouts  65.5 us (24%)
  matrix products  38.2 us (14%)
  blocking collectives  22.7 us (8%)
  between operations  15 us (6%)
  starting transfers between devices  14.9 us (5%)
  other arithmetic  6.71 us (2%)
    all_gather x1, waiting for transfers between devices, on_device(): lax.all_gather(w_down, 'ha', axis=1, tiled=True)  50.3 us
    all_gather x1, waiting for transfers between devices, on_device(): lax.all_gather(w_up, 'ha', axis=0, tiled=True)  28.4 us
    psum x1, waiting for transfers between devices, on_device(): summed = lax.psum(terms, 'col')  20.9 us
    all_to_all x1, blocking collectives, on_device(): lax.all_to_all(stacked, 'ta', split_axis=3, concat_axis=1, tiled=True)  19.9 us
    dot_general x1, matrix products, on_device(): jnp.dot(hidden, lax.all_gather(w_down, 'ha', axis=1, tiled=True), preferr...  12.3 us
    dot_general x3, matrix products, attend(): jnp.einsum('...qhd,...khd->...hqk', moved_q.reshape(split), moved_k.resha...  10.9 us
    dot_general x3, matrix products, attend(): jnp.einsum('...hqk,...khd->...qhd', weights, moved_v.reshape(split), pref...  10.2 us
    unnamed x5, waiting for transfers between devices  8.13 us
  transfers between devices with their start and end apart: 7, of which 4 were waited for; matrix products, arithmetic and copies ran while one was open for 29% of the time, Pallas kernels for 0%

commit v1 on v0

--- a/solution.py
+++ b/solution.py
@@ -6,6 +6,17 @@
 
 HD = 64
 EPS = 1e-05
+
+
+def run_pairs_all(mine, along_dim, local):
+    built, next_value = (mine.shape[:along_dim], mine.shape[along_dim + 1 :])
+    return jnp.moveaxis(mine.reshape(*built, local, -1, *next_value), along_dim, 0)
+
+
+def enter_the_skins(packet, dim_no):
+    packet = jnp.moveaxis(packet, 0, dim_no)
+    clean = packet.shape
+    return packet.reshape(*clean[:dim_no], clean[dim_no] * clean[dim_no + 1], *clean[dim_no + 2 :])
 
 
 def layer_norm(values, gain):
@@ -53,7 +64,14 @@
     along_w = attend(stacked[0], stacked[1], stacked[2], 2)
     columns = lax.all_to_all(stacked, "ha", split_axis=3, concat_axis=2, tiled=True)
     along_h_far = attend(columns[0], columns[1], columns[2], 1)
-    along_h = lax.all_to_all(along_h_far, "ha", split_axis=1, concat_axis=2, tiled=True)
+    block_next, arr_out = (lax.psum(1, "ha"), lax.axis_index("ha"))
+    b_next = run_pairs_all(along_h_far, 1, block_next)
+    samples = [b_next[arr_out]]
+    for q in [*range(1, block_next)]:
+        z_new = b_next[arr_out ^ q]
+        samples.append(lax.ppermute(z_new, "ha", [(kk, kk ^ q) for kk in range(block_next)]))
+    b_next = jnp.stack(samples, axis=0)[arr_out ^ jnp.arange(block_next)]
+    along_h = enter_the_skins(b_next, 2)
     lines = lax.all_to_all(stacked, "ta", split_axis=3, concat_axis=1, tiled=True)
     along_t_far = attend(lines[0], lines[1], lines[2], 0)
     along_t = lax.all_to_all(along_t_far, "ta", split_axis=0, concat_axis=2, tiled=True)

time: 272 us -> 258 us (0.949)
  blocking collectives: 22.7 us -> 2.78 us
  waiting for transfers between devices: 108 us -> 121 us
  local copies, waits for them, and re-layouts: 65.5 us -> 55.7 us
  starting transfers between devices: 14.9 us -> 18.8 us
    all_to_all x1 -> x0, blocking collectives: 19.9 us -> none  [on_device(): lax.all_to_all(stacked, 'ta', split_axis=3, concat_axis=1, tiled=True)]
    all_to_all x1, waiting for transfers between devices: 0.01 us -> 10.8 us  [on_device(): lax.all_to_all(stacked, 'ta', split_axis=3, concat_axis=1, tiled=True)]
    ppermute x0 -> x3, waiting for transfers between devices: none -> 4.5 us  [on_device(): lax.ppermute(z_new, 'ha', [(kk, kk ^ q) for kk in range(block_next)])]
    ppermute x0 -> x3, starting transfers between devices: none -> 4.39 us  [on_device(): lax.ppermute(z_new, 'ha', [(kk, kk ^ q) for kk in range(block_next)])]
  transfers between devices with their start and end apart: 7 -> 10, of which waited for: 4 -> 7; matrix products, arithmetic and copies ran while one was open for 29% -> 27% of each run, Pallas kernels for 0% -> 0%
where the time goes in v1:
time: 258 us; the launch traced here: 257 us
  waiting for transfers between devices  121 us (47%)
  local copies, waits for them, and re-layouts  55.7 us (22%)
  matrix products  36.4 us (14%)
  starting transfers between devices  18.8 us (7%)
  between operations  15.1 us (6%)
  other arithmetic  7.22 us (3%)
  blocking collectives  2.78 us (1%)
    all_gather x1, waiting for transfers between devices, on_device(): lax.all_gather(w_down, 'ha', axis=1, tiled=True)  50.2 us
    all_gather x1, waiting for transfers between devices, on_device(): lax.all_gather(w_up, 'ha', axis=0, tiled=True)  28.5 us
    psum x1, waiting for transfers between devices, on_device(): summed = lax.psum(terms, 'col')  19 us
    dot_general x1, matrix products, on_device(): jnp.dot(hidden, lax.all_gather(w_down, 'ha', axis=1, tiled=True), preferr...  11.4 us
    dot_general x3, matrix products, attend(): jnp.einsum('...qhd,...khd->...hqk', moved_q.reshape(split), moved_k.resha...  10.9 us
    all_to_all x1, waiting for transfers between devices, on_device(): lax.all_to_all(stacked, 'ta', split_axis=3, concat_axis=1, tiled=True)  10.8 us
    dot_general x3, matrix products, attend(): jnp.einsum('...hqk,...khd->...qhd', weights, moved_v.reshape(split), pref...  9.26 us
    unnamed x5, waiting for transfers between devices  8.13 us
  transfers between devices with their start and end apart: 10, of which 7 were waited for; matrix products, arithmetic and copies ran while one was open for 27% of the time, Pallas kernels for 0%

profile of v1, /device:TPU:0, one launch (start us, length us, event | category | flops | bytes accessed | tf_op | source)
XLA Modules:
  0.0 257.1 jit_solution(10478982688695002575)
XLA Ops:
  7.4 2.8 %all_gather.9 = bf16[2,4,64,768]{3,2,1,0:T(8,128)(2,1)S(1)} all-gather(bf16[2,4,64,384]{3,2,1,0:T(8,128)(2,1)} %param.7), channel_id=1, replica_groups=mesh['groups'=2,'ha'=4,'ta'=2,'col'=2] {'col'}, dimensions={3}, use_global_device_ids=true | all-gather | bytes 1179648 | tf_op jit(solution)/shard_map/all_gather | solution.py:54
  13.4 1.9 copy.134
  15.4 4.5 %all-to-all-start.1 = ((bf16[3,2,4,64,384]{4,2,1,0,3:T(4,128)(2,1)}), bf16[3,2,4,64,384]{4,2,1,0,3:T(4,128)(2,1)}, u32[]{:S(2)}, u32[]{:S(2)}) async-start(bf16[3,2,4,64,384]{4,2,1,0,3:T(4,128)(2,1)} %copy.134), calls=%async_computation.1 | async-start | bytes 2359296 | tf_op jit(solution)/shard_map/all_to_all | solution.py:75
  19.9 2.1 fusion.93
  22.0 2.4 reshape.166
  25.9 10.8 %all-to-all-done.1 = bf16[3,2,4,64,384]{4,2,1,0,3:T(4,128)(2,1)} async-done(((bf16[3,2,4,64,384]{4,2,1,0,3:T(4,128)(2,1)}), bf16[3,2,4,64,384]{4,2,1,0,3:T(4,128)(2,1)}, u32[]{:S(2)}, u32[]{:S(2)}) %all-to-all-start.1) | async-done | bytes 1179680 | tf_op jit(solution)/shard_map/all_to_all | solution.py:75
  36.6 5.1 %all-to-all-start = ((bf16[3,2,4,64,384]{4,2,1,0,3:T(4,128)(2,1)}), bf16[3,2,4,64,384]{4,2,1,0,3:T(4,128)(2,1)}, u32[]{:S(2)}, u32[]{:S(2)}) async-start(bf16[3,2,4,64,384]{4,2,1,0,3:T(4,128)(2,1)} %copy.134), calls=%async_computation | async-start | bytes 2359296 | tf_op jit(solution)/shard_map/all_to_all | solution.py:65
  41.8 3.3 %multiply_exponential_fusion.1 = f32[2,4,6,64,64]{3,4,2,1,0:T(8,128)} fusion(bf16[2,4,64,6,64]{4,3,2,1,0:T(8,128)(2,1)} %reshape.167, bf16[2,4,64,6,64]{4,3,2,1,0:T(8,128)(2,1)} %reshape.166), kind=kOutput, calls=%fused_computation.35 | convolution fusion | flops 25362432 | bytes 1572864 | tf_op jit(solution)/shard_map/...qhd,...khd->...hqk/dot_general | solution.py:37
  46.5 3.8 %convert_bitcast_fusion = f32[2,4,64,6,64]{2,4,3,1,0:T(8,128)} fusion(f32[2,4,6,64,64]{3,4,2,1,0:T(8,128)} %multiply_exponential_fusion.1, bf16[2,4,64,6,64]{4,3,2,1,0:T(8,128)(2,1)} %reshape.165), kind=kOutput, calls=%fused_computation.29 | convolution fusion | flops 25955392 | bytes 1966080 | tf_op jit(solution)/shard_map/...hqk,...khd->...qhd/dot_general | solution.py:47
  50.4 3.6 %copy.133 = f32[2,4,64,6,64]{2,1,0,4,3:T(4,128)} copy(f32[2,4,64,6,64]{2,4,3,1,0:T(8,128)} %convert_bitcast_fusion) | data formatting | bytes 1572864 | tf_op jit(solution)/shard_map/convert_element_type | solution.py:79
  54.0 3.1 %reshape.152 = f32[512,384]{0,1:T(8,128)} reshape(f32[2,4,64,6,64]{2,1,0,4,3:T(4,128)} %copy.133) | data formatting | bytes 1572864 | tf_op jit(solution)/shard_map/convert_element_type | solution.py:79
  59.5 2.4 reshape.172
  62.8 2.4 reshape.173
  65.1 3.8 %fusion.23 = f32[4,32,6,4,4]{3,4,2,1,0:T(4,128)} fusion(bf16[4,32,4,6,64]{4,3,1,0,2:T(8,128)(2,1)} %reshape.173, bf16[4,32,4,6,64]{4,3,1,0,2:T(8,128)(2,1)} %reshape.172), kind=kOutput, calls=%fused_computation.46 | convolution fusion | flops 1572864 | bytes 835584 | tf_op jit(solution)/shard_map/...qhd,...khd->...hqk/dot_general | solution.py:37
  69.0 1.9 copy.163
  74.3 2.4 fusion.21
  77.9 1.9 reshape.150
  80.5 4.2 %all-to-all-start.2 = ((bf16[4,4,32,384]{3,2,1,0:T(8,128)(2,1)}), bf16[4,4,32,384]{3,2,1,0:T(8,128)(2,1)}, u32[]{:S(2)}, u32[]{:S(2)}) async-start(bf16[4,4,32,384]{3,2,1,0:T(8,128)(2,1)} %copy.167), calls=%async_computation.2 | async-start | bytes 786432 | tf_op jit(solution)/shard_map/all_to_all | solution.py:77
  87.4 2.4 reshape.169
  90.6 2.4 reshape.170
  94.5 3.8 %multiply_exponential_fusion = f32[2,16,6,16,16]{3,4,2,1,0:T(8,128)} fusion(bf16[2,16,16,6,64]{4,3,1,2,0:T(8,128)(2,1)} %reshape.170, bf16[2,16,16,6,64]{4,3,1,2,0:T(8,128)(2,1)} %reshape.169), kind=kOutput, calls=%fused_computation.33 | convolution fusion | flops 6340608 | bytes 983040 | tf_op jit(solution)/shard_map/...qhd,...khd->...hqk/dot_general | solution.py:37
  98.4 3.0 %fusion.20 = bf16[2,16,16,6,64]{4,2,3,1,0:T(8,128)(2,1)S(1)} fusion(f32[2,16,6,16,16]{3,4,2,1,0:T(8,128)} %multiply_exponential_fusion, bf16[2,16,16,6,64]{4,3,1,2,0:T(8,128)(2,1)} %reshape.168), kind=kOutput, calls=%fused_computation.42 | convolution fusion | flops 6589455 | bytes 983040 | tf_op jit(solution)/shard_map/...hqk,...khd->...qhd/dot_general | solution.py:47
  105.4 2.0 collective-permute-start
  108.1 2.4 collective-permute-start.1
  113.4 3.2 %collective-permute-done.1 = bf16[2,4,16,384]{3,2,1,0:T(8,128)(2,1)} collective-permute-done((bf16[2,4,16,384]{3,2,1,0:T(8,128)(2,1)}, bf16[2,4,16,384]{3,2,1,0:T(8,128)(2,1)}, u32[]{:S(2)}, u32[]{:S(2)}) %collective-permute-start.1) | collective-permute-done | bytes 98336 | tf_op jit(solution)/shard_map/ppermute | solution.py:72
  120.9 3.6 %fusion.44 = f32[512,768]{1,0:T(8,128)} fusion(bf16[384,768]{1,0:T(8,128)(2,1)} %param.10, f32[512,384]{0,1:T(8,128)} %copy.169, f32[512,384]{0,1:T(8,128)} %reshape.152, f32[512,384]{0,1:T(8,128)} %copy.152), kind=kOutput, calls=%fused_computation.65 | convolution fusion | flops 302579712 | bytes 4521984 | tf_op jit(solution)/shard_map/dot_general | solution.py:81
  126.0 19.0 %all-reduce.2.cloned.1.call-done = f32[512,768]{1,0:T(8,128)} async-done(((f32[512,768]{1,0:T(8,128)}), f32[512,768]{1,0:T(8,128)}) %all-reduce.2.cloned.1.call-update) | async-done | bytes 1572880 | tf_op jit(solution)/shard_map/psum | solution.py:83
  148.1 28.5 %all-gather.3.cloned.1.call-done = bf16[768,1536]{1,0:T(8,128)(2,1)} async-done(((bf16[192,1536]{1,0:T(8,128)(2,1)}), bf16[768,1536]{1,0:T(8,128)(2,1)}) %all-gather.3.cloned.1.call-update) | async-done | bytes 2359312 | tf_op jit(solution)/shard_map/all_gather | solution.py:88
  176.6 50.2 %all-gather.5.cloned.1.call-done = bf16[1536,768]{0,1:T(8,128)(2,1)} async-done(((bf16[1536,192]{0,1:T(8,128)(2,1)}), bf16[1536,768]{0,1:T(8,128)(2,1)}) %all-gather.5.cloned.1.call-update) | async-done | bytes 2359312 | tf_op jit(solution)/shard_map/all_gather | solution.py:92
  226.8 11.4 %fusion.17 = bf16[512,768]{1,0:T(8,128)(2,1)S(1)} fusion(bf16[1536,768]{0,1:T(8,128)(2,1)} %all-gather.5.cloned.1.call-done, bf16[768,1536]{1,0:T(8,128)(2,1)} %all-gather.3.cloned.1.call-done, f32[512,768]{1,0:T(8,128)} %copy-done.1, f32[768]{0:T(1024)S(1)} %copy-done.4, f32[512]{0:T(512)S(1)} %add_rsqrt_fusion.1, f32[512]{0:T(512)S(1)} %broadcast_multiply_fusion.1), kind=kOutput, calls=%fused_computation.38 | convolution fusion | flops 2469003264 | bytes 7085056 | tf_op jit(solution)/shard_map/dot_general | solution.py:91
  239.4 7.0 %reduce-scatter.4.cloned.1.call-done = bf16[384,512]{1,0:T(8,128)(2,1)} async-done(((bf16[768,512]{1,0:T(8,128)(2,1)}), bf16[384,512]{1,0:T(8,128)(2,1)}) %reduce-scatter.4.cloned.1.call-update) | async-done | bytes 393232
  247.7 2.0 add_convert_fusion
  (74 shorter events, 38.7 us)
Async XLA Ops:
  7.4 3.8 %copy-start = (bf16[3,768,384]{2,1,0:T(8,128)(2,1)S(1)}, bf16[3,768,384]{2,1,0:T(8,128)(2,1)}, u32[]{:S(2)}) copy-start(bf16[3,768,384]{2,1,0:T(8,128)(2,1)} %param.9) | copy-start | bytes 5308420
  7.4 3.5 %copy-start.3 = (f32[768]{0:T(1024)S(1)}, f32[768]{0:T(1024)}, u32[]{:S(2)}) copy-start(f32[768]{0:T(1024)} %param.8) | copy-start | bytes 9220
  12.4 1.0 copy-start.2
  15.4 21.3 %all-to-all-start.1 = ((bf16[3,2,4,64,384]{4,2,1,0,3:T(4,128)(2,1)}), bf16[3,2,4,64,384]{4,2,1,0,3:T(4,128)(2,1)}, u32[]{:S(2)}, u32[]{:S(2)}) async-start(bf16[3,2,4,64,384]{4,2,1,0,3:T(4,128)(2,1)} %copy.134), calls=%async_computation.1 | async-start | bytes 2359296 | tf_op jit(solution)/shard_map/all_to_all | solution.py:75
  36.6 43.9 %all-to-all-start = ((bf16[3,2,4,64,384]{4,2,1,0,3:T(4,128)(2,1)}), bf16[3,2,4,64,384]{4,2,1,0,3:T(4,128)(2,1)}, u32[]{:S(2)}, u32[]{:S(2)}) async-start(bf16[3,2,4,64,384]{4,2,1,0,3:T(4,128)(2,1)} %copy.134), calls=%async_computation | async-start | bytes 2359296 | tf_op jit(solution)/shard_map/all_to_all | solution.py:65
  80.5 30.6 %all-to-all-start.2 = ((bf16[4,4,32,384]{3,2,1,0:T(8,128)(2,1)}), bf16[4,4,32,384]{3,2,1,0:T(8,128)(2,1)}, u32[]{:S(2)}, u32[]{:S(2)}) async-start(bf16[4,4,32,384]{3,2,1,0:T(8,128)(2,1)} %copy.167), calls=%async_computation.2 | async-start | bytes 786432 | tf_op jit(solution)/shard_map/all_to_all | solution.py:77
  84.7 60.3 %all-reduce.2.cloned.1.call-start = ((), (), s32[]{:S(2)}) async-start(), calls=%async_computation.4 | async-start | bytes 3145728 | tf_op jit(solution)/shard_map/psum | solution.py:83
  105.4 8.0 %collective-permute-start = (bf16[2,4,16,384]{3,2,1,0:T(8,128)(2,1)}, bf16[2,4,16,384]{3,2,1,0:T(8,128)(2,1)S(1)}, u32[]{:S(2)}, u32[]{:S(2)}) collective-permute-start(bf16[2,4,16,384]{3,2,1,0:T(8,128)(2,1)} %bitcast.113), channel_id=1, source_target_pairs={{0,4},{4,0},{8,12},{12,8},{1,5},{5,1},{9,13},{13,9},{2,6},{6,2},{1... | collective-permute-start | bytes 294920 | tf_op jit(solution)/shard_map/ppermute | solution.py:72
  108.1 8.6 %collective-permute-start.1 = (bf16[2,4,16,384]{3,2,1,0:T(8,128)(2,1)}, bf16[2,4,16,384]{3,2,1,0:T(8,128)(2,1)}, u32[]{:S(2)}, u32[]{:S(2)}) collective-permute-start(bf16[2,4,16,384]{3,2,1,0:T(8,128)(2,1)} %bitcast.112), channel_id=1, source_target_pairs={{0,8},{4,12},{8,0},{12,4},{1,9},{5,13},{9,1},{13,5},{2,10},{6,14},... | collective-permute-start | bytes 294920 | tf_op jit(solution)/shard_map/ppermute | solution.py:72
  111.1 6.8 %collective-permute-start.2 = (bf16[2,4,16,384]{3,2,1,0:T(8,128)(2,1)}, bf16[2,4,16,384]{3,2,1,0:T(8,128)(2,1)}, u32[]{:S(2)}, u32[]{:S(2)}) collective-permute-start(bf16[2,4,16,384]{3,2,1,0:T(8,128)(2,1)} %bitcast.111), channel_id=1, source_target_pairs={{0,12},{4,8},{8,4},{12,0},{1,13},{5,9},{9,5},{13,1},{2,14},{6,10},... | collective-permute-start | bytes 294920 | tf_op jit(solution)/shard_map/ppermute | solution.py:72
  124.5 52.1 %all-gather.3.cloned.1.call-start = ((), (), s32[]{:S(2)}) async-start(), calls=%async_computation.5 | async-start | bytes 2949120 | tf_op jit(solution)/shard_map/all_gather | solution.py:88
  125.1 101.7 %all-gather.5.cloned.1.call-start = ((), (), s32[]{:S(2)}) async-start(), calls=%async_computation.6 | async-start | bytes 2949120 | tf_op jit(solution)/shard_map/all_gather | solution.py:92
  125.7 101.1 %copy-start.4 = (f32[768]{0:T(1024)S(1)}, f32[768]{0:T(1024)}, u32[]{:S(2)}) copy-start(f32[768]{0:T(1024)} %param.11) | copy-start | bytes 9220
  125.7 120.8 %reduce-scatter.4.cloned.1.call-start = ((), (), s32[]{:S(2)}) async-start(), calls=%async_computation.7 | async-start | bytes 1179648
  146.6 1.2 copy-start.1
Sparse Core Ops, SparseCore 0:
  124.7 20.3 all-reduce.1
  239.6 6.8 reduce-scatter.3
Sparse Core Ops, SparseCore 1:
  126.7 49.9 all-gather.2
  178.1 48.6 all-gather.4
